TPU v7x, 32 devices: a whole 2x2x4 slice. The times are simulated.
32 devices in a mesh: field: 2 (over y), sky: 4 (over z), epoch: 2 (over x), vel: 2 (over core).
Axes of the slice: x: 2, y: 2, z: 4, core: 2. Of those that a mesh axis runs over, the one named last changes fastest.
Arguments:
- images: bfloat16 [64, 8, 128, 128], P(('epoch', 'vel'), ('field', 'sky')), parts along dimension 1, may hold values from -6 to 6
- variances: bfloat16 [64, 8, 128, 128], P(('epoch', 'vel'), ('field', 'sky')), parts along dimension 1, may hold values from 0.5 to 2
- valid: int32 [64, 8], P(('epoch', 'vel'), ('field', 'sky')), parts along dimension 1, may hold values from 0 to 1, as said below
- psf_sigma: float32 [128], P(('field', 'epoch', 'vel')), parts along dimension 0, may hold values from 0.8 to 2.5
- offsets: int32 [2, 16, 64], P(None, None, 'epoch'), may hold values from -12 to 12, as said below
Outputs:
- likelihood: float32 [16, 8, 128, 128], P(('epoch', 'vel'), ('field', 'sky')), parts along dimension 1
- flux: float32 [16, 8, 128, 128], P(('epoch', 'vel'), ('field', 'sky')), parts along dimension 1
There are 2 independent parts, one for each index of `field`. A program takes and returns all parts, laid end to end along the dimension named above; an argument that names none is the same for every part. Nothing has to cross between parts.
Inputs may be any that keep to these rules, and one draw needn't show every extreme that they name: Each hypothesis moves linearly: offsets[c, k, e] = floor(s[c, k] * e / 63) for integer speeds s within the range; both ends of the range are reached. `valid`: in one tile of the field, drawn from the seed, exactly one epoch is usable; in every other tile each frame is usable with probability 3/4, independently.
All inputs are finite; a program needn't handle non-finite values.
Results may differ from a plain program's by a relative error of at most 0.0058.
Values may be sent and summed in bfloat16 or wider, within the bound.
No kernel may reach another device: no remote copies, remote signals or barrier semaphores. Data moves between devices by JAX's collectives and lax.ppermute only.
A program may use at most 64 MiB of HBM per device.

v0:
```python
import functools

import jax
import jax.numpy as jnp
from jax import lax
from jax.experimental import pallas as pl
from jax.experimental.pallas import tpu as pltpu
from jax.sharding import PartitionSpec as P

VELS = 16
REACH = 12
PSFR = 7
GRID_X = 4

phi_floor = 0.25

F32 = jnp.float32
BF16 = jnp.bfloat16
EDGE = REACH + PSFR
PAD = 16
HALO = 32
SIDE = 48
HALF = 64
SPAN = 32
CHUNK = 4
STEP = 8


def iota(shape, axis):
    return lax.broadcasted_iota(jnp.int32, shape, axis)


def pick_edges(tile, first_left):
    row, lane = iota((2 * SIDE, tile), 0), iota((2 * SIDE, tile), 1)
    within = row % SIDE
    left = (row >= SIDE) != first_left
    wanted = within % EDGE + jnp.where(left, 0, SPAN + REACH) + jnp.where(within < EDGE, 0, HALF)
    return jnp.where((within < 2 * EDGE) & (lane == wanted), 1.0, 0.0).astype(BF16)


def segment_table(motion, epochs, first):
    code = (motion[0] + REACH) * 32 + motion[1] + REACH
    total = code.shape[1]
    lane = iota(code.shape, 1)
    later = jnp.roll(code, -1, axis=1) if total < 128 else pltpu.roll(code, total - 1, 1)
    stop = first + epochs
    end = jnp.where((later != code) | (lane == stop - 1), lane + 1, total)
    reach = 1
    while reach < epochs:
        end = jnp.minimum(end, jnp.where(lane + reach < total, jnp.roll(end, -reach, axis=1), total))
        reach *= 2
    return jnp.clip(end - first, 0, epochs) * 1024 + code


def over_segments(epochs, table_ref, maps_ref, chosen, slots, k_of, add):
    member = lax.axis_index("vel")
    row = iota((8, maps_ref.shape[-1]), 0)

    def segment(slot, e):
        word = table_ref[k_of(slot), member * epochs + e]
        e_end = word >> 10
        start = PAD - REACH + ((word >> 5) & 31)
        dx = (word & 31) - REACH
        tile = maps_ref.shape[-1]
        shift = jnp.where(dx > 0, tile - dx, -dx)
        base = pl.multiple_of((start // 8) * 8, 8)
        above = start - base
        turn = lax.rem(8 - above, 8)
        same = row < 8 - above
        put = add(slot, dx)

        def rows_at(r):
            window = pl.ds(base + r, 8)
            return [
                pltpu.roll(maps_ref[e_end, m, window] - maps_ref[e, m, window], turn, 0)
                for m in chosen
            ]

        upper = rows_at(0)
        for r in range(0, tile, 8):
            lower = rows_at(r + 8)
            put(r, [pltpu.roll(jnp.where(same, a, b), shift, 1) for a, b in zip(upper, lower)])
            upper = lower
        ended = e_end >= epochs
        return jnp.where(ended, jnp.minimum(slot + 1, slots), slot), jnp.where(ended, 0, e_end)

    def some_segments(state):
        for _ in range(STEP):
            state = segment(*state)
        return state

    start = (jnp.int32(0), jnp.int32(0))
    lax.while_loop(lambda state: state[0] < slots, some_segments, start)


def clear_sums(sum_ref):
    def clear(slot, carry):
        sum_ref[slot] = jnp.zeros(sum_ref.shape[1:], F32)
        return carry

    lax.fori_loop(0, sum_ref.shape[0] - 1, clear, 0)


def stack_edges(
    epochs, tile, block, n_epoch, n_vel, table_ref, maps_ref, sum_ref, send_ref, keep_ref
):
    column = lax.axis_index("epoch")
    member = lax.axis_index("vel")
    lane = iota((8, tile), 1)
    place = lane % SPAN - jnp.where(lane // SPAN % 2 == 0, REACH, 0)

    def add(slot, dx):
        held = (place + dx >= 0) & (place + dx < EDGE)

        def put(r, pieces):
            sum_ref[slot, r : r + 8] += jnp.where(held, pieces[0], 0.0)

        return put

    first_k = (column + 1) * n_vel * block
    over_segments(
        epochs, table_ref, maps_ref, (0,), VELS, lambda slot: lax.rem(first_k + slot, VELS), add
    )

    selector = pick_edges(tile, member == 1)

    def pack(group, carry):
        for i in range(block):
            slot = group * block + i
            packed = lax.dot_general(
                selector, sum_ref[slot].astype(BF16), (((1,), (1,)), ((), ())),
                preferred_element_type=F32,
            )
            rows = pl.ds(slot * SIDE, SIDE)
            keep_ref[rows] = packed[:SIDE]
            send_ref[rows] = packed[SIDE:].astype(BF16)
        return carry

    lax.fori_loop(0, VELS // block, pack, 0)


def main_kernel(epochs, tile, block, n_epoch, n_vel, ranks, sent, kept, table_ref, maps_ref, *refs):
    sum_ref = refs[-1]
    clear_sums(sum_ref)
    column = lax.axis_index("epoch")
    member = lax.axis_index("vel")
    lane = iota((8, tile), 1)
    turned = (lane + HALF) % tile
    share = (ranks[1] - ranks[0]) * block
    slots = (sent + kept) * share

    def k_of(slot):
        whose = jnp.where(slot < sent * share, 1 - member, member)
        rank = ranks[0] + lax.rem(slot, share) // block
        owner = lax.rem(column + 1 + rank, n_epoch)
        return (owner * n_vel + whose) * block + lax.rem(slot, block)

    def add(slot, dx):
        out = (lane + dx < 0) | (lane + dx >= tile)
        out_turned = (turned + dx < 0) | (turned + dx >= tile)

        def put(r, pieces):
            psi, phi, side = pieces
            sum_ref[slot, 0, r : r + 8] += jnp.where(out, side, psi)
            sum_ref[slot, 1, r : r + 8] += jnp.where(out_turned, side, phi)

        return put

    over_segments(epochs, table_ref, maps_ref, (0, 1, 2), slots, k_of, add)

    def write(target_ref, first):
        def one(j, carry):
            rows = pl.ds(j * 2 * tile, 2 * tile)
            value = sum_ref[first + j].reshape(2 * tile, tile)
            target_ref[rows] = value.astype(target_ref.dtype)
            return carry

        lax.fori_loop(0, share, one, 0)

    if sent:
        write(refs[0], 0)
    if kept:
        write(refs[sent], sent * share)


def stack_kernel(
    epochs, tile, block, n_epoch, n_vel, prepared,
    taken_ref, sigma_hbm, valid_hbm, motion_hbm, first_hbm, second_hbm,
    send_ref, keep_ref, maps_ref, coded_ref,
    sigma_ref, valid_ref, motion_ref, table_ref, first_ref, second_ref, edges_ref, sum_ref,
    small_sems, data_sems, table_sem,
):
    height = tile + 2 * PAD
    chunks = epochs // CHUNK
    member = lax.axis_index("vel")

    small = [
        pltpu.make_async_copy(motion_hbm, motion_ref, small_sems.at[0]),
        pltpu.make_async_copy(sigma_hbm, sigma_ref, small_sems.at[1]),
        pltpu.make_async_copy(valid_hbm, valid_ref, small_sems.at[2]),
    ]
    for copy in small:
        copy.start()

    def data_copy(c, i):
        at = pl.ds(c * CHUNK, CHUNK)
        source, target = ((first_hbm, first_ref), (second_hbm, second_ref))[i]
        return pltpu.make_async_copy(source.at[at], target.at[at], data_sems.at[2 * c + i])

    for c in range(chunks):
        for i in range(2):
            data_copy(c, i).start()

    row, lane = iota((tile, tile), 0), iota((tile, tile), 1)
    gap = jnp.abs(row - lane)
    ring = jnp.minimum(gap, tile - gap)
    outside = ring > PSFR
    far = gap >= tile // 2
    ring = ring.astype(F32)

    def edge_distance(first_row):
        at, ln = iota((SPAN, tile), 0) + first_row, iota((SPAN, tile), 1)
        left, place = ln // SPAN % 2 == 0, ln % SPAN
        source = place + jnp.where(left, -EDGE, tile - REACH)
        place = place - jnp.where(left, REACH, 0)
        away = jnp.abs(at - source)
        return away.astype(F32), (away > PSFR) | (place < 0) | (place >= EDGE)

    edge_gaps = [edge_distance(0), edge_distance(tile - SPAN)]
    of_psi = iota((SPAN, tile), 1) < HALF
    if prepared:
        depth = tile + 2 * HALO
        drop = jnp.abs(iota((height, depth), 1) - HALO - iota((height, depth), 0) + PAD)
        dropped = drop > PSFR
        drop = drop.astype(F32)

    maps_ref[0] = jnp.zeros(maps_ref.shape[1:], F32)
    edges_ref[0] = jnp.zeros(edges_ref.shape[1:], F32)
    clear_sums(sum_ref)
    for copy in small:
        copy.wait()
    coded_ref[...] = segment_table(motion_ref[...], epochs, member * epochs)
    table = pltpu.make_async_copy(coded_ref, table_ref, table_sem)
    table.start()

    def weights(e):
        def profile(distance, beyond):
            scaled = distance * (1.0 / jnp.full((1, distance.shape[1]), sigma_ref[e], F32))
            return jnp.where(beyond, 0.0, jnp.exp(-0.5 * (scaled * scaled)))

        turned = profile(ring, outside)
        scale = 1.0 / jnp.sum(turned[:8], axis=1, keepdims=True)[:1]
        turned = turned * scale
        bands = profile(drop, dropped) * scale if prepared else None
        ends = [profile(*gap) * scale for gap in edge_gaps]
        result = []
        blank = jnp.zeros((tile - 2 * PAD, tile), F32)
        for m in range(2):
            value = turned if m == 0 else turned * turned
            inside = jnp.where(far, 0.0, value)
            beyond = jnp.where(far, value, 0.0)
            top, bottom = beyond[:PAD], beyond[tile - PAD :]
            if prepared:
                band = (bands if m == 0 else bands * bands).astype(BF16)
            else:
                band = jnp.concatenate([bottom, inside, top], axis=0).astype(BF16)
            if m == 1:
                inside, top, bottom = (pltpu.roll(v, HALF, 1) for v in (inside, top, bottom))
            outer = jnp.concatenate([top, blank, bottom], axis=0)
            if m == 0:
                first, last = (jnp.where(of_psi, end, 0.0) for end in ends)
            else:
                first, last = (jnp.where(of_psi, 0.0, end * end) for end in ends)
            gap_rows = jnp.zeros((tile - 2 * SPAN, tile), F32)
            edge = jnp.concatenate([first, gap_rows, last], axis=0)
            result.append((band, *(v.astype(BF16) for v in (inside, outer, edge))))
        return result

    def correlate(e):
        if prepared:
            pair = first_ref[e], second_ref[e]
        else:
            inverse = valid_ref[e].astype(F32) / second_ref[e].astype(F32)
            pair = (first_ref[e].astype(F32) * inverse).astype(BF16), inverse.astype(BF16)
        (band, inside, outer, edge), (band2, inside2, outer2, edge2) = weights(e)

        def apart(a, b):
            wide = [jnp.concatenate([a, jnp.zeros_like(a)], axis=1)]
            wide.append(jnp.concatenate([jnp.zeros_like(b), b], axis=1))
            return jnp.concatenate(wide, axis=0)

        rows = jnp.dot(
            jnp.concatenate([band, band2], axis=1), apart(*pair), preferred_element_type=F32
        ).astype(BF16)
        maps = jnp.dot(rows, apart(inside, inside2), preferred_element_type=F32)
        sides = jnp.dot(
            rows,
            jnp.concatenate(
                [
                    jnp.concatenate([outer, edge], axis=1),
                    jnp.concatenate([outer2, edge2], axis=1),
                ],
                axis=0,
            ),
            preferred_element_type=F32,
        )
        return maps[:, :tile], maps[:, tile:], sides[:, :tile], sides[:, tile:]

    def correlate_chunk(c, carry):
        for i in range(2):
            data_copy(c, i).wait()
        made = [correlate(c * CHUNK + u) for u in range(CHUNK)]
        for i in range(4):
            held, at = (maps_ref, i) if i < 3 else (edges_ref, 0)
            total = held[c * CHUNK, at]
            for u in range(CHUNK):
                total = total + made[u][i]
                held[c * CHUNK + u + 1, at] = total
        return carry

    lax.fori_loop(0, chunks, correlate_chunk, 0)
    table.wait()
    stack_edges(
        epochs, tile, block, n_epoch, n_vel, table_ref, edges_ref, sum_ref, send_ref, keep_ref
    )


def join_kernel(keep_ref, arrived_ref, own_ref, *refs):
    beyond, (far_ref, side_ref) = refs[:-2], refs[-2:]
    far_ref[...] = (keep_ref[...] + arrived_ref[...].astype(F32)).astype(BF16)
    side = own_ref[...].astype(F32)
    for edge_ref in beyond:
        side = side + edge_ref[...].astype(F32)
    side_ref[...] = side.astype(BF16)


def finish_kernel(tile, block, keep_ref, own_ref, both_ref, *refs):
    mains, (like_hbm, flux_hbm, like_ref, flux_ref, sems) = refs[:-5], refs[-5:]
    copies = []
    row, lane = iota((SIDE, tile), 0), iota((SIDE, tile), 1)
    member = lax.axis_index("vel")
    placed = []
    for m in range(2):
        at = row - m * EDGE
        used = (at >= 0) & (at < EDGE)
        for right in (1 - member, member):
            wanted = at + jnp.where(right == 1, 0, tile - EDGE) + m * HALF
            placed.append(jnp.where(used & (lane == wanted % tile), 1.0, 0.0).astype(BF16))
    for i in range(block):
        sums = []
        for m in range(2):
            rows = slice((2 * i + m) * tile, (2 * i + m + 1) * tile)
            total = keep_ref[rows] + own_ref[rows].astype(F32)
            for main_ref in mains:
                total = total + main_ref[rows].astype(F32)
            for near, put in enumerate(placed[2 * m : 2 * m + 2]):
                at = (near * block + i) * SIDE
                total = total + lax.dot_general(
                    both_ref[at : at + SIDE], put, (((0,), (0,)), ((), ())),
                    preferred_element_type=F32,
                )
            sums.append(total)
        root = lax.rsqrt(jnp.maximum(pltpu.roll(sums[1], HALF, 1), phi_floor))
        like = sums[0] * root
        like_ref[i] = like
        flux_ref[i] = like * root
        for j, (source, target) in enumerate(((like_ref, like_hbm), (flux_ref, flux_hbm))):
            copies.append(pltpu.make_async_copy(source.at[i], target.at[i], sems.at[2 * i + j]))
            copies[-1].start()
    for copy in copies:
        copy.wait()


def move(block, axis, distance):
    count = lax.axis_size(axis)
    return lax.ppermute(block, axis, [(i, (i + distance) % count) for i in range(count)])


def beside(block, step, keep):
    count = lax.axis_size("sky")
    device = [(q - GRID_X // 2) % count for q in range(count)]
    route = [(device[q], device[q + step]) for q in range(count) if keep(q)]
    return lax.ppermute(block, "sky", route)


def beside_by_member(block):
    n_sky = lax.axis_size("sky")
    device = [(q - GRID_X // 2) % n_sky for q in range(n_sky)]
    route = []
    for q in range(n_sky):
        for v, step in ((0, 1), (1, -1)):
            if 0 <= q % GRID_X + step < GRID_X:
                route.append((device[q] * 2 + v, device[q + step] * 2 + v))
    return lax.ppermute(block, ("sky", "vel"), route)


def on_device(images, variances, valid, psf_sigma, offsets):
    epochs, tile = images.shape[0], images.shape[-1]
    n_epoch, n_vel = lax.axis_size("epoch"), lax.axis_size("vel")
    n_sky = lax.axis_size("sky")
    assert n_vel == 2 and epochs % CHUNK == 0
    block = VELS // (n_epoch * n_vel)
    first, second = images[:, 0], variances[:, 0]
    prepared = n_sky > GRID_X
    if prepared:
        usable = valid[:, 0].astype(F32)[:, None, None]
        scaled = (first.astype(F32) / second.astype(F32) * usable).astype(BF16)
        inverse = (usable / second.astype(F32)).astype(BF16)
        pair = jnp.stack([scaled, inverse])
        above = beside(pair[:, :, tile - HALO :], GRID_X, lambda q: q + GRID_X < n_sky)
        below = beside(pair[:, :, :HALO], -GRID_X, lambda q: q >= GRID_X)
        first, second = jnp.concatenate([above, pair, below], axis=2)

    main_rows = block * 2 * tile
    edge_rows = block * SIDE
    hbm = pl.BlockSpec(memory_space=pltpu.HBM)
    vmem = pl.BlockSpec(memory_space=pltpu.VMEM)
    params = pltpu.CompilerParams(vmem_limit_bytes=16 * 1024 * 1024)
    small_params = pltpu.CompilerParams(vmem_limit_bytes=8 * 1024 * 1024)
    group_rows = n_vel * edge_rows
    operands = (psf_sigma, valid[:, 0], offsets, first, second)
    taken = lax.axis_index("sky") < n_sky
    flag = taken.astype(jnp.int32)[None]
    send_edges, keep_edges, maps, table = pl.pallas_call(
        functools.partial(stack_kernel, epochs, tile, block, n_epoch, n_vel, prepared),
        out_shape=(
            jax.ShapeDtypeStruct((n_epoch * group_rows, tile), BF16),
            jax.ShapeDtypeStruct((n_epoch * group_rows, tile), F32),
            jax.ShapeDtypeStruct((epochs + 1, 3, tile + 2 * PAD, tile), F32),
            jax.ShapeDtypeStruct(offsets.shape[1:], jnp.int32),
        ),
        in_specs=[pl.BlockSpec(memory_space=pltpu.SMEM)] + [hbm] * 5,
        out_specs=(vmem,) * 4,
        scratch_shapes=[
            pltpu.SMEM((epochs,), F32),
            pltpu.SMEM((epochs,), jnp.int32),
            pltpu.VMEM(offsets.shape, jnp.int32),
            pltpu.SMEM(offsets.shape[1:], jnp.int32),
            pltpu.VMEM(first.shape, BF16),
            pltpu.VMEM(second.shape, BF16),
            pltpu.VMEM((epochs + 1, 1, tile + 2 * PAD, tile), F32),
            pltpu.VMEM((VELS + 1, tile, tile), F32),
            pltpu.SemaphoreType.DMA((3,)),
            pltpu.SemaphoreType.DMA((2 * (epochs // CHUNK),)),
            pltpu.SemaphoreType.DMA,
        ],
        compiler_params=params,
    )(flag, *(pltpu.with_memory_space_constraint(a, pltpu.HBM) for a in operands))
    edges = (keep_edges + move(send_edges, "vel", 1).astype(F32)).astype(BF16)
    beyond = [
        move(edges[(d - 1) * group_rows : d * group_rows], "epoch", d) for d in range(1, n_epoch)
    ]

    def main_sums(ranks, sent, kept, maps, hand_on):
        rows = (ranks[1] - ranks[0]) * main_rows
        results = [jax.ShapeDtypeStruct((rows, tile), BF16)] * sent
        results += [jax.ShapeDtypeStruct((rows, tile), F32)] * kept
        aliases = {1: len(results)} if hand_on else {}
        results += [jax.ShapeDtypeStruct(maps.shape, F32)] * hand_on
        slots = (sent + kept) * (ranks[1] - ranks[0]) * block
        return pl.pallas_call(
            functools.partial(
                main_kernel, epochs, tile, block, n_epoch, n_vel, ranks, sent, kept
            ),
            out_shape=results,
            in_specs=[pl.BlockSpec(memory_space=pltpu.SMEM), vmem],
            out_specs=[vmem] * len(results),
            input_output_aliases=aliases,
            scratch_shapes=[pltpu.VMEM((slots + 1, 2, tile, tile), F32)],
            compiler_params=small_params,
        )(table, maps)

    far_ranks, own_ranks = (0, n_epoch - 1), (n_epoch - 1, n_epoch)
    send, maps = main_sums(far_ranks, 1, 0, maps, 1)
    keep, maps = main_sums(far_ranks, 0, 1, maps, 1)
    far, side = pl.pallas_call(
        join_kernel,
        out_shape=(
            jax.ShapeDtypeStruct(keep.shape, BF16),
            jax.ShapeDtypeStruct((group_rows, tile), BF16),
        ),
        in_specs=[vmem] * (3 + len(beyond)),
        out_specs=(vmem, vmem),
        compiler_params=small_params,
    )(keep, move(send, "vel", 1), edges[(n_epoch - 1) * group_rows :], *beyond)
    side = beside_by_member(side)
    mains = [
        move(far[(d - 1) * main_rows : d * main_rows], "epoch", d) for d in range(1, n_epoch)
    ]

    def pass_own(send, side):
        arrived = move(send, "vel", 1)
        is_first = lax.axis_index("vel") == 0
        near = jnp.where(is_first, side[:edge_rows], side[edge_rows:])
        other = jnp.where(is_first, side[edge_rows:], side[:edge_rows])
        return arrived, jnp.concatenate([near, move(other, "vel", 1)])

    send, keep = main_sums(own_ranks, 1, 1, maps, 0)
    arrived, side = lax.cond(taken, pass_own, lambda send, side: (send, side), send, side)

    shape = jax.ShapeDtypeStruct((block, tile, tile), F32)
    likelihood, flux = pl.pallas_call(
        functools.partial(finish_kernel, tile, block),
        out_shape=(shape, shape),
        in_specs=[vmem] * (3 + len(mains)),
        out_specs=(hbm, hbm),
        scratch_shapes=[
            pltpu.VMEM(shape.shape, F32),
            pltpu.VMEM(shape.shape, F32),
            pltpu.SemaphoreType.DMA((2 * block,)),
        ],
        compiler_params=params,
    )(keep, arrived, side, *mains)
    return likelihood[:, None], flux[:, None]


def solution(mesh):
    placed = (
        P(("epoch", "vel"), ("field", "sky"), None, None),
        P(("epoch", "vel"), ("field", "sky"), None, None),
        P(("epoch", "vel"), ("field", "sky")),
        P(("field", "epoch", "vel")),
        P(None, None, "epoch"),
    )
    return jax.shard_map(
        on_device,
        mesh=mesh,
        in_specs=placed,
        out_specs=(
            P(("epoch", "vel"), ("field", "sky"), None, None),
            P(("epoch", "vel"), ("field", "sky"), None, None),
        ),
        check_vma=False,
    )
```

profile of v0, /device:TPU:0, one launch (start us, length us, event | category | flops | bytes accessed | tf_op | source)
XLA Modules:
  0.0 30.5 jit_solution(11108560585601460823)
XLA Ops:
  0.6 8.0 %shard_map.68 = (bf16[768,128]{1,0:T(8,128)(2,1)S(1)}, f32[768,128]{1,0:T(8,128)S(1)}, f32[17,3,160,128]{3,2,1,0:T(8,128)S(1)}, s32[16,32]{1,0:T(8,128)S(1)}) custom-call(s32[1]{0:T(128)} %bitcast.taken_ref, f32[16]{0:T(128)} %sigma_hbm.1, s32[16]{0:T(128)} %bitcast.12, s32[2,16,32]{2,1,0:T(8,128)} %motion_hbm.1, bf16[16,128,128]{2,1,0:T(8,128)(2,1)} %bitcast.10, ...), custom_call_target="tpu_custom_call" | custom-call | tf_op jit(solution)/shard_map/pallas_call | solution.py:424
  8.7 0.5 %collective-permute-start.3 = (bf16[768,128]{1,0:T(8,128)(2,1)S(1)}, bf16[768,128]{1,0:T(8,128)(2,1)S(1)}, u32[]{:S(2)}, u32[]{:S(2)}) collective-permute-start(bf16[768,128]{1,0:T(8,128)(2,1)S(1)} %get-tuple-element.37), channel_id=1, source_target_pairs={{0,1},{1,0},{2,3},{3,2},{4,5},{5,4},{6,7},{7,6},{8,9},{9,8},{10,11... | collective-permute-start | bytes 589832 | tf_op jit(solution)/shard_map/ppermute | solution.py:376
  9.2 1.8 %shard_map.69 = (bf16[1024,128]{1,0:T(8,128)(2,1)S(1)}, f32[17,3,160,128]{3,2,1,0:T(8,128)S(1)}) custom-call(s32[16,32]{1,0:T(8,128)S(1)} %get-tuple-element.28.table_ref, f32[17,3,160,128]{3,2,1,0:T(8,128)S(1)} %get-tuple-element.29.maps_ref), custom_call_target="tpu_custom_call", output_to_operand_aliasing={{1}: (1, {})} | custom-call | tf_op jit(solution)/shard_map/pallas_call | solution.py:461
  11.0 0.1 collective-permute-start.2
  11.1 0.0 collective-permute-done.3
  11.1 0.1 add_convert_fusion
  11.2 3.3 %collective-permute-start.4 = (bf16[384,128]{1,0:T(8,128)(2,1)S(1)}, bf16[384,128]{1,0:T(8,128)(2,1)S(1)}, u32[]{:S(2)}, u32[]{:S(2)}) collective-permute-start(bf16[384,128]{1,0:T(8,128)(2,1)S(1)} %get-tuple-element.48), channel_id=1, source_target_pairs={{0,2},{2,0},{1,3},{3,1},{4,6},{6,4},{5,7},{7,5},{8,10},{10,8},{9,1... | collective-permute-start | bytes 294920 | tf_op jit(solution)/shard_map/ppermute | solution.py:376
  14.5 1.8 %shard_map.70 = (f32[1024,128]{1,0:T(8,128)S(1)}, f32[17,3,160,128]{3,2,1,0:T(8,128)S(1)}) custom-call(s32[16,32]{1,0:T(8,128)S(1)} %get-tuple-element.28.table_ref, f32[17,3,160,128]{3,2,1,0:T(8,128)S(1)} %get-tuple-element.30.maps_ref), custom_call_target="tpu_custom_call", output_to_operand_aliasing={{1}: (1, {})} | custom-call | tf_op jit(solution)/shard_map/pallas_call | solution.py:461
  16.2 0.0 collective-permute-done.2.arrived_ref
  16.3 1.2 %collective-permute-done.4.refs_0_ = bf16[384,128]{1,0:T(8,128)(2,1)S(1)} collective-permute-done((bf16[384,128]{1,0:T(8,128)(2,1)S(1)}, bf16[384,128]{1,0:T(8,128)(2,1)S(1)}, u32[]{:S(2)}, u32[]{:S(2)}) %collective-permute-start.4) | collective-permute-done | bytes 98336 | tf_op jit(solution)/shard_map/ppermute | solution.py:376
  17.4 0.1 shard_map.72
  17.5 1.8 %collective-permute-start.6 = (bf16[1024,128]{1,0:T(8,128)(2,1)S(1)}, bf16[1024,128]{1,0:T(8,128)(2,1)S(1)}, u32[]{:S(2)}, u32[]{:S(2)}) collective-permute-start(bf16[1024,128]{1,0:T(8,128)(2,1)S(1)} %get-tuple-element.41), channel_id=1, source_target_pairs={{0,2},{2,0},{1,3},{3,1},{4,6},{6,4},{5,7},{7,5},{8,10},{10,8},{9,1... | collective-permute-start | bytes 786440 | tf_op jit(solution)/shard_map/ppermute | solution.py:376
  19.4 3.5 %collective-permute-start.5 = (bf16[384,128]{1,0:T(8,128)(2,1)S(1)}, bf16[384,128]{1,0:T(8,128)(2,1)S(1)}, u32[]{:S(2)}, u32[]{:S(2)}) collective-permute-start(bf16[384,128]{1,0:T(8,128)(2,1)S(1)} %get-tuple-element.38), channel_id=1, source_target_pairs={{8,12},{12,0},{13,9},{0,4},{1,13},{5,1},{10,14},{14,2},{15,11},{2,... | collective-permute-start | bytes 294920 | tf_op jit(solution)/shard_map/ppermute | solution.py:394
  22.8 3.4 %shard_map.71 = (bf16[1024,128]{1,0:T(8,128)(2,1)S(1)}, f32[1024,128]{1,0:T(8,128)S(1)}) custom-call(s32[16,32]{1,0:T(8,128)S(1)} %get-tuple-element.28.table_ref, f32[17,3,160,128]{3,2,1,0:T(8,128)S(1)} %get-tuple-element.31.maps_ref), custom_call_target="tpu_custom_call" | custom-call | tf_op jit(solution)/shard_map/pallas_call | solution.py:461
  26.2 1.4 %collective-permute-done.5 = bf16[384,128]{1,0:T(8,128)(2,1)S(1)} collective-permute-done((bf16[384,128]{1,0:T(8,128)(2,1)S(1)}, bf16[384,128]{1,0:T(8,128)(2,1)S(1)}, u32[]{:S(2)}, u32[]{:S(2)}) %collective-permute-start.5) | collective-permute-done | bytes 98336 | tf_op jit(solution)/shard_map/ppermute | solution.py:394
  27.6 1.6 %conditional.1 = ((bf16[1024,128]{1,0:T(8,128)(2,1)S(1)}, bf16[384,128]{1,0:T(8,128)(2,1)S(1)})) conditional(s32[]{:T(128)} %convert_element_type.10, (bf16[1024,128]{1,0:T(8,128)(2,1)S(1)}, bf16[384,128]{1,0:T(8,128)(2,1)S(1)}) %tuple.15, (bf16[1024,128]{1,0:T(8,128)(2,1)S(1)}, bf16[384,128]{1,0:T(8,128)(2,1)S(1)}) %tuple.15), branch_computations={%region_0.0_spmd, %region_1.2_spmd} | conditional | flops 245763 | bytes 2162822 | solution.py:499
  27.6 0.0 collective-permute-start
  27.7 0.6 %collective-permute-start.1 = (bf16[192,128]{1,0:T(8,128)(2,1)S(1)}, bf16[192,128]{1,0:T(8,128)(2,1)S(1)}, u32[]{:S(2)}, u32[]{:S(2)}) collective-permute-start(bf16[192,128]{1,0:T(8,128)(2,1)S(1)} %get-tuple-element.47), channel_id=1, source_target_pairs={{0,1},{1,0},{2,3},{3,2},{4,5},{5,4},{6,7},{7,6},{8,9},{9,8},{10,11... | collective-permute-start | bytes 147464 | tf_op jit(solution)/shard_map/cond/branch_1_fun/ppermute | solution.py:376
  28.2 1.0 %collective-permute-done.1 = bf16[192,128]{1,0:T(8,128)(2,1)S(1)} collective-permute-done((bf16[192,128]{1,0:T(8,128)(2,1)S(1)}, bf16[192,128]{1,0:T(8,128)(2,1)S(1)}, u32[]{:S(2)}, u32[]{:S(2)}) %collective-permute-start.1) | collective-permute-done | bytes 49184 | tf_op jit(solution)/shard_map/cond/branch_1_fun/ppermute | solution.py:376
  29.3 0.0 collective-permute-done
  29.3 0.0 collective-permute-done.6.refs_0_
  29.3 1.2 %shard_map.73 = (f32[4,128,128]{2,1,0:T(8,128)}, f32[4,128,128]{2,1,0:T(8,128)}) custom-call(f32[1024,128]{1,0:T(8,128)S(1)} %get-tuple-element.32.keep_ref, bf16[1024,128]{1,0:T(8,128)(2,1)S(1)} %get-tuple-element.39.own_ref, bf16[384,128]{1,0:T(8,128)(2,1)S(1)} %get-tuple-element.40.both_ref, bf16[1024,128]{1,0:T(8,128)(2,1)S(1)} %collective-permute-done.6.refs_0_), custom_call_target="tpu_custom_call" | custom-call | tf_op jit(solution)/shard_map/pallas_call | solution.py:502
  (4 shorter events, 0.1 us)
Async XLA Ops:
  8.7 2.4 %collective-permute-start.3 = (bf16[768,128]{1,0:T(8,128)(2,1)S(1)}, bf16[768,128]{1,0:T(8,128)(2,1)S(1)}, u32[]{:S(2)}, u32[]{:S(2)}) collective-permute-start(bf16[768,128]{1,0:T(8,128)(2,1)S(1)} %get-tuple-element.37), channel_id=1, source_target_pairs={{0,1},{1,0},{2,3},{3,2},{4,5},{5,4},{6,7},{7,6},{8,9},{9,8},{10,11... | collective-permute-start | bytes 589832 | tf_op jit(solution)/shard_map/ppermute | solution.py:376
  11.0 5.3 %collective-permute-start.2 = (bf16[1024,128]{1,0:T(8,128)(2,1)S(1)}, bf16[1024,128]{1,0:T(8,128)(2,1)S(1)}, u32[]{:S(2)}, u32[]{:S(2)}) collective-permute-start(bf16[1024,128]{1,0:T(8,128)(2,1)S(1)} %get-tuple-element.35), channel_id=1, source_target_pairs={{0,1},{1,0},{2,3},{3,2},{4,5},{5,4},{6,7},{7,6},{8,9},{9,8},{10,11... | collective-permute-start | bytes 786440 | tf_op jit(solution)/shard_map/ppermute | solution.py:376
  11.2 6.3 %collective-permute-start.4 = (bf16[384,128]{1,0:T(8,128)(2,1)S(1)}, bf16[384,128]{1,0:T(8,128)(2,1)S(1)}, u32[]{:S(2)}, u32[]{:S(2)}) collective-permute-start(bf16[384,128]{1,0:T(8,128)(2,1)S(1)} %get-tuple-element.48), channel_id=1, source_target_pairs={{0,2},{2,0},{1,3},{3,1},{4,6},{6,4},{5,7},{7,5},{8,10},{10,8},{9,1... | collective-permute-start | bytes 294920 | tf_op jit(solution)/shard_map/ppermute | solution.py:376
  17.5 11.8 %collective-permute-start.6 = (bf16[1024,128]{1,0:T(8,128)(2,1)S(1)}, bf16[1024,128]{1,0:T(8,128)(2,1)S(1)}, u32[]{:S(2)}, u32[]{:S(2)}) collective-permute-start(bf16[1024,128]{1,0:T(8,128)(2,1)S(1)} %get-tuple-element.41), channel_id=1, source_target_pairs={{0,2},{2,0},{1,3},{3,1},{4,6},{6,4},{5,7},{7,5},{8,10},{10,8},{9,1... | collective-permute-start | bytes 786440 | tf_op jit(solution)/shard_map/ppermute | solution.py:376
  19.4 8.3 %collective-permute-start.5 = (bf16[384,128]{1,0:T(8,128)(2,1)S(1)}, bf16[384,128]{1,0:T(8,128)(2,1)S(1)}, u32[]{:S(2)}, u32[]{:S(2)}) collective-permute-start(bf16[384,128]{1,0:T(8,128)(2,1)S(1)} %get-tuple-element.38), channel_id=1, source_target_pairs={{8,12},{12,0},{13,9},{0,4},{1,13},{5,1},{10,14},{14,2},{15,11},{2,... | collective-permute-start | bytes 294920 | tf_op jit(solution)/shard_map/ppermute | solution.py:394
  27.6 1.6 %collective-permute-start = (bf16[1024,128]{1,0:T(8,128)(2,1)S(1)}, bf16[1024,128]{1,0:T(8,128)(2,1)S(1)}, u32[]{:S(2)}, u32[]{:S(2)}) collective-permute-start(bf16[1024,128]{1,0:T(8,128)(2,1)S(1)} %get-tuple-element.8), channel_id=1, source_target_pairs={{0,1},{1,0},{2,3},{3,2},{4,5},{5,4},{6,7},{7,6},{8,9},{9,8},{10,11... | collective-permute-start | bytes 786440 | tf_op jit(solution)/shard_map/cond/branch_1_fun/ppermute | solution.py:376
  27.7 1.6 %collective-permute-start.1 = (bf16[192,128]{1,0:T(8,128)(2,1)S(1)}, bf16[192,128]{1,0:T(8,128)(2,1)S(1)}, u32[]{:S(2)}, u32[]{:S(2)}) collective-permute-start(bf16[192,128]{1,0:T(8,128)(2,1)S(1)} %get-tuple-element.47), channel_id=1, source_target_pairs={{0,1},{1,0},{2,3},{3,2},{4,5},{5,4},{6,7},{7,6},{8,9},{9,8},{10,11... | collective-permute-start | bytes 147464 | tf_op jit(solution)/shard_map/cond/branch_1_fun/ppermute | solution.py:376
where the time goes:
time: 30.3 us; the launch traced here: 30.5 us
  Pallas kernels  16.2 us (53%)
  starting transfers between devices  9.77 us (32%)
  waiting for transfers between devices  3.62 us (12%)
  between operations  0.71 us (2%)
    pallas_call x1, Pallas kernels, on_device(): pl.pallas_call(functools.partial(stack_kernel, epochs, tile, block, n_epo...  8.05 us
    pallas_call x3, Pallas kernels, main_sums(): pl.pallas_call(functools.partial(main_kernel, epochs, tile, block, n_epoc...  6.95 us
    ppermute x6, starting transfers between devices, move(): lax.ppermute(block, axis, [(i, (i + distance) % count) for i in range(cou...  6.3 us
    ppermute x1, starting transfers between devices, beside_by_member(): return lax.ppermute(block, ('sky', 'vel'), route)  3.47 us
    ppermute x6, waiting for transfers between devices, move(): lax.ppermute(block, axis, [(i, (i + distance) % count) for i in range(cou...  2.22 us
    ppermute x1, waiting for transfers between devices, beside_by_member(): return lax.ppermute(block, ('sky', 'vel'), route)  1.4 us
    pallas_call x1, Pallas kernels, on_device(): pl.pallas_call(functools.partial(finish_kernel, tile, block), out_shape=(...  1.15 us
  transfers between devices with their start and end apart: 7, of which 3 were waited for; matrix products, arithmetic and copies ran while one was open for 0% of the time, Pallas kernels for 23%

commit v1 on v0

--- a/solution.py
+++ b/solution.py
@@ -24,6 +24,8 @@
 SPAN = 32
 CHUNK = 4
 STEP = 8
+EDGE_STEP = 16
+PIECE = 11
 
 
 def iota(shape, axis):
@@ -52,7 +54,7 @@
     return jnp.clip(end - first, 0, epochs) * 1024 + code
 
 
-def over_segments(epochs, table_ref, maps_ref, chosen, slots, k_of, add):
+def over_segments(epochs, table_ref, maps_ref, chosen, slots, k_of, step, add):
     member = lax.axis_index("vel")
     row = iota((8, maps_ref.shape[-1]), 0)
 
@@ -85,7 +87,7 @@
         return jnp.where(ended, jnp.minimum(slot + 1, slots), slot), jnp.where(ended, 0, e_end)
 
     def some_segments(state):
-        for _ in range(STEP):
+        for _ in range(step):
             state = segment(*state)
         return state
 
@@ -119,7 +121,8 @@
 
     first_k = (column + 1) * n_vel * block
     over_segments(
-        epochs, table_ref, maps_ref, (0,), VELS, lambda slot: lax.rem(first_k + slot, VELS), add
+        epochs, table_ref, maps_ref, (0,), VELS, lambda slot: lax.rem(first_k + slot, VELS),
+        EDGE_STEP, add,
     )
 
     selector = pick_edges(tile, member == 1)
@@ -166,7 +169,7 @@
 
         return put
 
-    over_segments(epochs, table_ref, maps_ref, (0, 1, 2), slots, k_of, add)
+    over_segments(epochs, table_ref, maps_ref, (0, 1, 2), slots, k_of, STEP, add)
 
     def write(target_ref, first):
         def one(j, carry):
@@ -351,8 +354,15 @@
         for m in range(2):
             rows = slice((2 * i + m) * tile, (2 * i + m + 1) * tile)
             total = keep_ref[rows] + own_ref[rows].astype(F32)
-            for main_ref in mains:
-                total = total + main_ref[rows].astype(F32)
+            for main_ref, rest_ref in zip(mains[: len(mains) // 2], mains[len(mains) // 2 :]):
+                cut = main_ref.shape[0]
+                split = min(max(cut, rows.start), rows.stop)
+                held = []
+                if split > rows.start:
+                    held.append(main_ref[rows.start : split])
+                if split < rows.stop:
+                    held.append(rest_ref[split - cut : rows.stop - cut])
+                total = total + jnp.concatenate([h.astype(F32) for h in held], axis=0)
             for near, put in enumerate(placed[2 * m : 2 * m + 2]):
                 at = (near * block + i) * SIDE
                 total = total + lax.dot_general(
@@ -484,9 +494,12 @@
         compiler_params=small_params,
     )(keep, move(send, "vel", 1), edges[(n_epoch - 1) * group_rows :], *beyond)
     side = beside_by_member(side)
-    mains = [
-        move(far[(d - 1) * main_rows : d * main_rows], "epoch", d) for d in range(1, n_epoch)
-    ]
+    piece = main_rows * PIECE // 16
+    mains, rests = [], []
+    for d in range(1, n_epoch):
+        at = (d - 1) * main_rows
+        mains.append(move(far[at : at + piece], "epoch", d))
+        rests.append(move(far[at + piece : at + main_rows], "epoch", d))
 
     def pass_own(send, side):
         arrived = move(send, "vel", 1)
@@ -502,7 +515,7 @@
     likelihood, flux = pl.pallas_call(
         functools.partial(finish_kernel, tile, block),
         out_shape=(shape, shape),
-        in_specs=[vmem] * (3 + len(mains)),
+        in_specs=[vmem] * (3 + 2 * len(mains)),
         out_specs=(hbm, hbm),
         scratch_shapes=[
             pltpu.VMEM(shape.shape, F32),
@@ -510,7 +523,7 @@
             pltpu.SemaphoreType.DMA((2 * block,)),
         ],
         compiler_params=params,
-    )(keep, arrived, side, *mains)
+    )(keep, arrived, side, *mains, *rests)
     return likelihood[:, None], flux[:, None]
 
 

time: 30.3 us -> 30.2 us (level); the launches traced: 30.5 us -> 29.7 us
  Pallas kernels: 16.2 us -> 15.4 us
    pallas_call x3, Pallas kernels: 6.95 us -> 6.44 us  [main_sums(): pl.pallas_call(functools.partial(main_kernel, epochs, tile, block, n_epoc...]
    pallas_call x1, Pallas kernels: 8.05 us -> 7.74 us  [on_device(): pl.pallas_call(functools.partial(stack_kernel, epochs, tile, block, n_epo...]
    ppermute x6 -> x7, waiting for transfers between devices: 2.22 us -> 2.43 us  [move(): lax.ppermute(block, axis, [(i, (i + distance) % count) for i in range(cou...]
    ppermute x6 -> x7, starting transfers between devices: 6.3 us -> 6.41 us  [move(): lax.ppermute(block, axis, [(i, (i + distance) % count) for i in range(cou...]
  transfers between devices with their start and end apart: 7 -> 8, of which waited for: 3 -> 3; matrix products, arithmetic and copies ran while one was open for 0% -> 0% of each run, Pallas kernels for 23% -> 22%
where the time goes in v1:
time: 30.2 us; the launch traced here: 29.7 us
  Pallas kernels  15.4 us (51%)
  starting transfers between devices  9.88 us (33%)
  waiting for transfers between devices  3.54 us (12%)
  between operations  0.74 us (2%)
    pallas_call x1, Pallas kernels, on_device(): pl.pallas_call(functools.partial(stack_kernel, epochs, tile, block, n_epo...  7.74 us
    pallas_call x3, Pallas kernels, main_sums(): pl.pallas_call(functools.partial(main_kernel, epochs, tile, block, n_epoc...  6.44 us
    ppermute x7, starting transfers between devices, move(): lax.ppermute(block, axis, [(i, (i + distance) % count) for i in range(cou...  6.41 us
    ppermute x1, starting transfers between devices, beside_by_member(): return lax.ppermute(block, ('sky', 'vel'), route)  3.47 us
    ppermute x7, waiting for transfers between devices, move(): lax.ppermute(block, axis, [(i, (i + distance) % count) for i in range(cou...  2.43 us
    pallas_call x1, Pallas kernels, on_device(): pl.pallas_call(functools.partial(finish_kernel, tile, block), out_shape=(...  1.16 us
    ppermute x1, waiting for transfers between devices, beside_by_member(): return lax.ppermute(block, ('sky', 'vel'), route)  1.11 us
  transfers between devices with their start and end apart: 8, of which 3 were waited for; matrix products, arithmetic and copies ran while one was open for 0% of the time, Pallas kernels for 22%

profile of v1, /device:TPU:0, one launch (start us, length us, event | category | flops | bytes accessed | tf_op | source)
XLA Modules:
  0.0 29.7 jit_solution(11895373235131188217)
XLA Ops:
  0.6 7.7 %shard_map.68 = (bf16[768,128]{1,0:T(8,128)(2,1)S(1)}, f32[768,128]{1,0:T(8,128)S(1)}, f32[17,3,160,128]{3,2,1,0:T(8,128)S(1)}, s32[16,32]{1,0:T(8,128)S(1)}) custom-call(s32[1]{0:T(128)} %bitcast.taken_ref, f32[16]{0:T(128)} %sigma_hbm.1, s32[16]{0:T(128)} %bitcast.12, s32[2,16,32]{2,1,0:T(8,128)} %motion_hbm.1, bf16[16,128,128]{2,1,0:T(8,128)(2,1)} %bitcast.10, ...), custom_call_target="tpu_custom_call" | custom-call | tf_op jit(solution)/shard_map/pallas_call | solution.py:434
  8.4 0.1 collective-permute-start.3
  8.5 1.8 %shard_map.69 = (bf16[1024,128]{1,0:T(8,128)(2,1)S(1)}, f32[17,3,160,128]{3,2,1,0:T(8,128)S(1)}) custom-call(s32[16,32]{1,0:T(8,128)S(1)} %get-tuple-element.28.table_ref, f32[17,3,160,128]{3,2,1,0:T(8,128)S(1)} %get-tuple-element.29.maps_ref), custom_call_target="tpu_custom_call", output_to_operand_aliasing={{1}: (1, {})} | custom-call | tf_op jit(solution)/shard_map/pallas_call | solution.py:471
  10.3 0.5 %collective-permute-start.2 = (bf16[1024,128]{1,0:T(8,128)(2,1)S(1)}, bf16[1024,128]{1,0:T(8,128)(2,1)S(1)}, u32[]{:S(2)}, u32[]{:S(2)}) collective-permute-start(bf16[1024,128]{1,0:T(8,128)(2,1)S(1)} %get-tuple-element.35), channel_id=1, source_target_pairs={{0,1},{1,0},{2,3},{3,2},{4,5},{5,4},{6,7},{7,6},{8,9},{9,8},{10,11... | collective-permute-start | bytes 786440 | tf_op jit(solution)/shard_map/ppermute | solution.py:386
  10.8 0.0 collective-permute-done.3
  10.8 0.1 add_convert_fusion
  10.9 2.6 %collective-permute-start.4 = (bf16[384,128]{1,0:T(8,128)(2,1)S(1)}, bf16[384,128]{1,0:T(8,128)(2,1)S(1)}, u32[]{:S(2)}, u32[]{:S(2)}) collective-permute-start(bf16[384,128]{1,0:T(8,128)(2,1)S(1)} %get-tuple-element.48), channel_id=1, source_target_pairs={{0,2},{2,0},{1,3},{3,1},{4,6},{6,4},{5,7},{7,5},{8,10},{10,8},{9,1... | collective-permute-start | bytes 294920 | tf_op jit(solution)/shard_map/ppermute | solution.py:386
  13.5 1.8 %shard_map.70 = (f32[1024,128]{1,0:T(8,128)S(1)}, f32[17,3,160,128]{3,2,1,0:T(8,128)S(1)}) custom-call(s32[16,32]{1,0:T(8,128)S(1)} %get-tuple-element.28.table_ref, f32[17,3,160,128]{3,2,1,0:T(8,128)S(1)} %get-tuple-element.30.maps_ref), custom_call_target="tpu_custom_call", output_to_operand_aliasing={{1}: (1, {})} | custom-call | tf_op jit(solution)/shard_map/pallas_call | solution.py:471
  15.3 0.0 collective-permute-done.2.arrived_ref
  15.3 1.4 %collective-permute-done.4.refs_0_ = bf16[384,128]{1,0:T(8,128)(2,1)S(1)} collective-permute-done((bf16[384,128]{1,0:T(8,128)(2,1)S(1)}, bf16[384,128]{1,0:T(8,128)(2,1)S(1)}, u32[]{:S(2)}, u32[]{:S(2)}) %collective-permute-start.4) | collective-permute-done | bytes 98336 | tf_op jit(solution)/shard_map/ppermute | solution.py:386
  16.7 0.1 shard_map.72
  16.8 1.8 %collective-permute-start.6 = (bf16[704,128]{1,0:T(8,128)(2,1)S(1)}, bf16[704,128]{1,0:T(8,128)(2,1)S(1)}, u32[]{:S(2)}, u32[]{:S(2)}) collective-permute-start(bf16[704,128]{1,0:T(8,128)(2,1)S(1)} %slice.22), channel_id=1, source_target_pairs={{0,2},{2,0},{1,3},{3,1},{4,6},{6,4},{5,7},{7,5},{8,10},{10,8},{9,1... | collective-permute-start | bytes 540680 | tf_op jit(solution)/shard_map/ppermute | solution.py:386
  18.6 3.5 %collective-permute-start.5 = (bf16[384,128]{1,0:T(8,128)(2,1)S(1)}, bf16[384,128]{1,0:T(8,128)(2,1)S(1)}, u32[]{:S(2)}, u32[]{:S(2)}) collective-permute-start(bf16[384,128]{1,0:T(8,128)(2,1)S(1)} %get-tuple-element.38), channel_id=1, source_target_pairs={{8,12},{12,0},{13,9},{0,4},{1,13},{5,1},{10,14},{14,2},{15,11},{2,... | collective-permute-start | bytes 294920 | tf_op jit(solution)/shard_map/ppermute | solution.py:404
  22.1 0.8 %collective-permute-start.7 = (bf16[320,128]{1,0:T(8,128)(2,1)S(1)}, bf16[320,128]{1,0:T(8,128)(2,1)S(1)}, u32[]{:S(2)}, u32[]{:S(2)}) collective-permute-start(bf16[320,128]{1,0:T(8,128)(2,1)S(1)} %slice.23), channel_id=1, source_target_pairs={{0,2},{2,0},{1,3},{3,1},{4,6},{6,4},{5,7},{7,5},{8,10},{10,8},{9,1... | collective-permute-start | bytes 245768 | tf_op jit(solution)/shard_map/ppermute | solution.py:386
  22.9 2.9 %shard_map.71 = (bf16[1024,128]{1,0:T(8,128)(2,1)S(1)}, f32[1024,128]{1,0:T(8,128)S(1)}) custom-call(s32[16,32]{1,0:T(8,128)S(1)} %get-tuple-element.28.table_ref, f32[17,3,160,128]{3,2,1,0:T(8,128)S(1)} %get-tuple-element.31.maps_ref), custom_call_target="tpu_custom_call" | custom-call | tf_op jit(solution)/shard_map/pallas_call | solution.py:471
  25.8 1.1 %collective-permute-done.5 = bf16[384,128]{1,0:T(8,128)(2,1)S(1)} collective-permute-done((bf16[384,128]{1,0:T(8,128)(2,1)S(1)}, bf16[384,128]{1,0:T(8,128)(2,1)S(1)}, u32[]{:S(2)}, u32[]{:S(2)}) %collective-permute-start.5) | collective-permute-done | bytes 98336 | tf_op jit(solution)/shard_map/ppermute | solution.py:404
  26.9 1.6 %conditional.1 = ((bf16[1024,128]{1,0:T(8,128)(2,1)S(1)}, bf16[384,128]{1,0:T(8,128)(2,1)S(1)})) conditional(s32[]{:T(128)} %convert_element_type.10, (bf16[1024,128]{1,0:T(8,128)(2,1)S(1)}, bf16[384,128]{1,0:T(8,128)(2,1)S(1)}) %tuple.15, (bf16[1024,128]{1,0:T(8,128)(2,1)S(1)}, bf16[384,128]{1,0:T(8,128)(2,1)S(1)}) %tuple.15), branch_computations={%region_0.0_spmd, %region_1.2_spmd} | conditional | flops 245763 | bytes 2162822 | solution.py:512
  26.9 0.0 collective-permute-start
  26.9 0.6 %collective-permute-start.1 = (bf16[192,128]{1,0:T(8,128)(2,1)S(1)}, bf16[192,128]{1,0:T(8,128)(2,1)S(1)}, u32[]{:S(2)}, u32[]{:S(2)}) collective-permute-start(bf16[192,128]{1,0:T(8,128)(2,1)S(1)} %get-tuple-element.47), channel_id=1, source_target_pairs={{0,1},{1,0},{2,3},{3,2},{4,5},{5,4},{6,7},{7,6},{8,9},{9,8},{10,11... | collective-permute-start | bytes 147464 | tf_op jit(solution)/shard_map/cond/branch_1_fun/ppermute | solution.py:386
  27.5 1.0 %collective-permute-done.1 = bf16[192,128]{1,0:T(8,128)(2,1)S(1)} collective-permute-done((bf16[192,128]{1,0:T(8,128)(2,1)S(1)}, bf16[192,128]{1,0:T(8,128)(2,1)S(1)}, u32[]{:S(2)}, u32[]{:S(2)}) %collective-permute-start.1) | collective-permute-done | bytes 49184 | tf_op jit(solution)/shard_map/cond/branch_1_fun/ppermute | solution.py:386
  28.5 0.0 collective-permute-done
  28.6 0.0 collective-permute-done.7.refs_1_
  28.6 0.0 collective-permute-done.6.refs_0_
  28.6 1.2 %shard_map.73 = (f32[4,128,128]{2,1,0:T(8,128)}, f32[4,128,128]{2,1,0:T(8,128)}) custom-call(f32[1024,128]{1,0:T(8,128)S(1)} %get-tuple-element.32.keep_ref, bf16[1024,128]{1,0:T(8,128)(2,1)S(1)} %get-tuple-element.39.own_ref, bf16[384,128]{1,0:T(8,128)(2,1)S(1)} %get-tuple-element.40.both_ref, bf16[704,128]{1,0:T(8,128)(2,1)S(1)} %collective-permute-done.6.refs_0_, ...), custom_call_target="tpu_custom_call" | custom-call | tf_op jit(solution)/shard_map/pallas_call | solution.py:515
  (6 shorter events, 0.1 us)
Async XLA Ops:
  8.4 2.4 %collective-permute-start.3 = (bf16[768,128]{1,0:T(8,128)(2,1)S(1)}, bf16[768,128]{1,0:T(8,128)(2,1)S(1)}, u32[]{:S(2)}, u32[]{:S(2)}) collective-permute-start(bf16[768,128]{1,0:T(8,128)(2,1)S(1)} %get-tuple-element.37), channel_id=1, source_target_pairs={{0,1},{1,0},{2,3},{3,2},{4,5},{5,4},{6,7},{7,6},{8,9},{9,8},{10,11... | collective-permute-start | bytes 589832 | tf_op jit(solution)/shard_map/ppermute | solution.py:386
  10.3 5.0 %collective-permute-start.2 = (bf16[1024,128]{1,0:T(8,128)(2,1)S(1)}, bf16[1024,128]{1,0:T(8,128)(2,1)S(1)}, u32[]{:S(2)}, u32[]{:S(2)}) collective-permute-start(bf16[1024,128]{1,0:T(8,128)(2,1)S(1)} %get-tuple-element.35), channel_id=1, source_target_pairs={{0,1},{1,0},{2,3},{3,2},{4,5},{5,4},{6,7},{7,6},{8,9},{9,8},{10,11... | collective-permute-start | bytes 786440 | tf_op jit(solution)/shard_map/ppermute | solution.py:386
  10.9 5.8 %collective-permute-start.4 = (bf16[384,128]{1,0:T(8,128)(2,1)S(1)}, bf16[384,128]{1,0:T(8,128)(2,1)S(1)}, u32[]{:S(2)}, u32[]{:S(2)}) collective-permute-start(bf16[384,128]{1,0:T(8,128)(2,1)S(1)} %get-tuple-element.48), channel_id=1, source_target_pairs={{0,2},{2,0},{1,3},{3,1},{4,6},{6,4},{5,7},{7,5},{8,10},{10,8},{9,1... | collective-permute-start | bytes 294920 | tf_op jit(solution)/shard_map/ppermute | solution.py:386
  16.8 11.8 %collective-permute-start.6 = (bf16[704,128]{1,0:T(8,128)(2,1)S(1)}, bf16[704,128]{1,0:T(8,128)(2,1)S(1)}, u32[]{:S(2)}, u32[]{:S(2)}) collective-permute-start(bf16[704,128]{1,0:T(8,128)(2,1)S(1)} %slice.22), channel_id=1, source_target_pairs={{0,2},{2,0},{1,3},{3,1},{4,6},{6,4},{5,7},{7,5},{8,10},{10,8},{9,1... | collective-permute-start | bytes 540680 | tf_op jit(solution)/shard_map/ppermute | solution.py:386
  18.6 8.3 %collective-permute-start.5 = (bf16[384,128]{1,0:T(8,128)(2,1)S(1)}, bf16[384,128]{1,0:T(8,128)(2,1)S(1)}, u32[]{:S(2)}, u32[]{:S(2)}) collective-permute-start(bf16[384,128]{1,0:T(8,128)(2,1)S(1)} %get-tuple-element.38), channel_id=1, source_target_pairs={{8,12},{12,0},{13,9},{0,4},{1,13},{5,1},{10,14},{14,2},{15,11},{2,... | collective-permute-start | bytes 294920 | tf_op jit(solution)/shard_map/ppermute | solution.py:404
  22.1 6.5 %collective-permute-start.7 = (bf16[320,128]{1,0:T(8,128)(2,1)S(1)}, bf16[320,128]{1,0:T(8,128)(2,1)S(1)}, u32[]{:S(2)}, u32[]{:S(2)}) collective-permute-start(bf16[320,128]{1,0:T(8,128)(2,1)S(1)} %slice.23), channel_id=1, source_target_pairs={{0,2},{2,0},{1,3},{3,1},{4,6},{6,4},{5,7},{7,5},{8,10},{10,8},{9,1... | collective-permute-start | bytes 245768 | tf_op jit(solution)/shard_map/ppermute | solution.py:386
  26.9 1.6 %collective-permute-start = (bf16[1024,128]{1,0:T(8,128)(2,1)S(1)}, bf16[1024,128]{1,0:T(8,128)(2,1)S(1)}, u32[]{:S(2)}, u32[]{:S(2)}) collective-permute-start(bf16[1024,128]{1,0:T(8,128)(2,1)S(1)} %get-tuple-element.8), channel_id=1, source_target_pairs={{0,1},{1,0},{2,3},{3,2},{4,5},{5,4},{6,7},{7,6},{8,9},{9,8},{10,11... | collective-permute-start | bytes 786440 | tf_op jit(solution)/shard_map/cond/branch_1_fun/ppermute | solution.py:386
  26.9 1.6 %collective-permute-start.1 = (bf16[192,128]{1,0:T(8,128)(2,1)S(1)}, bf16[192,128]{1,0:T(8,128)(2,1)S(1)}, u32[]{:S(2)}, u32[]{:S(2)}) collective-permute-start(bf16[192,128]{1,0:T(8,128)(2,1)S(1)} %get-tuple-element.47), channel_id=1, source_target_pairs={{0,1},{1,0},{2,3},{3,2},{4,5},{5,4},{6,7},{7,6},{8,9},{9,8},{10,11... | collective-permute-start | bytes 147464 | tf_op jit(solution)/shard_map/cond/branch_1_fun/ppermute | solution.py:386
